TPU v7x, 1024 devices: a whole 4x8x16 slice. The times are simulated.
1024 devices in a mesh: row: 64 (over y, x, core), col: 16 (over z).
Axes of the slice: x: 4, y: 8, z: 16, core: 2. Of those that a mesh axis runs over, the one named last changes fastest.
Arguments:
- features: bfloat16 [65536, 128], P(('row', 'col')), may hold values from -6 to 6
- degrees: int32 [65536], P('row'), may hold values from 1 to 4
- tiles: bfloat16 [1024, 16, 128, 128], P(('row', 'col')), may hold values from -0.09375 to 0.09375
- tile_slots: int32 [1024, 16], P(('row', 'col')), may hold values from 0 to 255, as said below
- tile_counts: int32 [1024], P(('row', 'col')), may hold values from 4 to 16, as said below
- w_first: bfloat16 [128, 256], replicated, may hold values from -0.5 to 0.5
- w_second: bfloat16 [256, 172], replicated, may hold values from -0.375 to 0.375
- cotangent: bfloat16 [65536, 172], P('row'), may hold values from -6 to 6
Outputs:
- logits: bfloat16 [65536, 172], P(('row', 'col'))
- grad_first: float32 [128, 256], replicated
- grad_second: float32 [256, 172], replicated
Inputs may be any that keep to these rules, and one draw needn't show every extreme that they name: `tile_slots`: each row lists 16 distinct tile positions of its device's block of 8 x 32 tiles. `tile_counts`: some device uses all 16 slots.
All inputs are finite; a program needn't handle non-finite values.
Results may differ from a plain program's by a relative error of at most 0.007.
Values may be sent and summed in bfloat16 or wider, within the bound.
A program may use at most 32 MiB of HBM per device.

v0:
```python
import jax
import jax.numpy as jnp
from jax import lax
from jax.sharding import PartitionSpec as P


def gelu_plain(value):
    return jax.nn.gelu(value, approximate=True)


def gelu_slope(value):
    return jax.jvp(gelu_plain, (value,), (jnp.ones_like(value),))[1]


def shards(features, degrees, tiles, tile_slots, tile_counts, w_first, w_second, cotangent):
    col_count = lax.axis_size("col")
    row_count = lax.axis_size("row")
    node_rows = features.shape[0]
    col_place = lax.axis_index("col")
    slot_total = tiles.shape[1]
    tile_rows = col_count * node_rows // 128
    tile_cols = row_count * node_rows // 128
    stripe_scale = lax.rsqrt(degrees.astype(jnp.float32))
    own_scale = lax.dynamic_slice_in_dim(stripe_scale, col_place * node_rows, node_rows)[:, None]
    block_tiles = tiles[0]
    slots_here = tile_slots[0]
    live_mask = (jnp.arange(slot_total) < tile_counts[0]).astype(jnp.float32)
    row_of = slots_here // tile_cols
    col_of = slots_here % tile_cols
    row_pick = (jnp.arange(tile_rows)[:, None] == row_of[None, :]).astype(jnp.float32) * live_mask[
        None, :
    ]
    col_pick = (jnp.arange(tile_cols)[:, None] == col_of[None, :]).astype(jnp.float32) * live_mask[
        None, :
    ]

    def aggregate(source):
        width = source.shape[-1]
        gathered = lax.all_gather(source, "row", axis=0, tiled=True)
        blocks = gathered.reshape(tile_cols, 128, width)[col_of]
        prods = jnp.einsum("tij,tjf->tif", block_tiles, blocks, preferred_element_type=jnp.float32)
        partial_rows = jnp.einsum("rt,tif->rif", row_pick, prods, precision=lax.Precision.HIGHEST)
        summed = lax.psum_scatter(
            partial_rows.reshape(tile_rows * 128, width), "col", scatter_dimension=0, tiled=True
        )
        return own_scale * summed

    scaled_in = (own_scale * features.astype(jnp.float32)).astype(jnp.bfloat16)
    first_agg = aggregate(scaled_in).astype(jnp.bfloat16)
    first_pre = jnp.dot(first_agg, w_first, preferred_element_type=jnp.float32)
    scaled_hidden = (own_scale * gelu_plain(first_pre)).astype(jnp.bfloat16)
    second_agg = aggregate(scaled_hidden).astype(jnp.bfloat16)
    logits = jnp.dot(second_agg, w_second, preferred_element_type=jnp.float32).astype(jnp.bfloat16)
    own_cot = lax.dynamic_slice_in_dim(cotangent, col_place * node_rows, node_rows)
    grad_second = jnp.dot(second_agg.T, own_cot, preferred_element_type=jnp.float32)
    scaled_cot = (stripe_scale[:, None] * cotangent.astype(jnp.float32)).astype(jnp.bfloat16)
    cls_width = scaled_cot.shape[-1]
    cot_blocks = scaled_cot.reshape(tile_rows, 128, cls_width)[row_of]
    prods = jnp.einsum("tij,tif->tjf", block_tiles, cot_blocks, preferred_element_type=jnp.float32)
    terms = jnp.einsum("ct,tjf->cjf", col_pick, prods, precision=lax.Precision.HIGHEST)
    narrow = lax.psum_scatter(
        terms.reshape(tile_cols * 128, cls_width), "row", scatter_dimension=0, tiled=True
    )
    back_sum = jnp.dot(narrow, w_second.astype(jnp.float32).T, precision=lax.Precision.HIGHEST)
    grad_hidden = own_scale * back_sum
    grad_pre = (grad_hidden * gelu_slope(first_pre)).astype(jnp.bfloat16)
    grad_first = jnp.dot(first_agg.T, grad_pre, preferred_element_type=jnp.float32)
    grad_first, grad_second = lax.psum((grad_first, grad_second), ("row", "col"))
    return (logits, grad_first, grad_second)


def solution(mesh):
    placed = (
        P(("row", "col"), None),
        P("row"),
        P(("row", "col"), None, None, None),
        P(("row", "col"), None),
        P(("row", "col")),
        P(),
        P(),
        P("row", None),
    )
    return jax.shard_map(
        shards,
        mesh=mesh,
        in_specs=placed,
        out_specs=(P(("row", "col"), None), P(), P()),
        check_vma=False,
    )
```

profile of v0, /device:TPU:1, one launch (start us, length us, event | category | flops | bytes accessed | tf_op | source)
XLA Modules:
  0.0 1028.5 jit_solution(15235751590539489113)
XLA Ops:
  7.2 0.7 convert_rsqrt_fusion
  8.0 1.4 multiply_convert_fusion.4
  11.5 103.0 %all-gather.3.cloned.1.call-done = bf16[4096,128]{1,0:T(8,128)(2,1)} async-done(((bf16[64,128]{1,0:T(8,128)(2,1)}), bf16[4096,128]{1,0:T(8,128)(2,1)}) %all-gather.3.cloned.1.call-update) | async-done | bytes 1048592 | tf_op jit(solution)/shard_map/all_gather | solution.py:39
  114.5 1.9 gather_fusion
  118.1 0.9 copy.30
  119.1 60.6 %reduce-scatter.6.cloned.1.call-done = f32[64,128]{1,0:T(8,128)} async-done(((f32[1024,128]{1,0:T(8,128)}), f32[64,128]{1,0:T(8,128)}) %reduce-scatter.6.cloned.1.call-update) | async-done | bytes 32784 | tf_op jit(solution)/shard_map/reduce_scatter | solution.py:43
  179.7 1.6 multiply_convert_fusion.2
  182.8 2.6 fusion
  185.4 3.3 copy.40
  188.8 98.1 %all-gather.5.cloned.1.call-done = bf16[4096,256]{1,0:T(8,128)(2,1)} async-done(((bf16[64,256]{1,0:T(8,128)(2,1)}), bf16[4096,256]{1,0:T(8,128)(2,1)}) %all-gather.5.cloned.1.call-update) | async-done | bytes 2097168 | tf_op jit(solution)/shard_map/all_gather | solution.py:39
  286.9 3.2 gather_fusion.1
  290.1 1.7 convolution_bitcast_fusion
  291.8 2.1 copy.32
  293.9 2.7 fusion.21
  296.6 1.3 copy.33
  298.0 156.6 %reduce-scatter.10.cloned.1.call-done = f32[64,172]{1,0:T(8,128)} async-done(((f32[4096,172]{1,0:T(8,128)}), f32[64,172]{1,0:T(8,128)}) %reduce-scatter.10.cloned.1.call-update) | async-done | bytes 44048
  454.6 1.0 fusion.3
  455.7 0.9 fusion.44
  456.6 69.6 %reduce-scatter.8.cloned.1.call-done = f32[64,256]{1,0:T(8,128)} async-done(((f32[1024,256]{1,0:T(8,128)}), f32[64,256]{1,0:T(8,128)}) %reduce-scatter.8.cloned.1.call-update) | async-done | bytes 65552 | tf_op jit(solution)/shard_map/reduce_scatter | solution.py:43
  526.2 1.7 fusion.17
  527.9 1.6 convolution_convert_fusion
  529.6 488.9 %all-reduce.3.cloned.1.call-done = (f32[128,256]{1,0:T(8,128)}, f32[256,172]{0,1:T(8,128)}) async-done(((f32[128,256]{1,0:T(8,128)}, f32[256,172]{0,1:T(8,128)}), (f32[128,256]{1,0:T(8,128)}, f32[256,172]{0,1:T(8,128)})) %all-reduce.3.cloned.1.call-update) | async-done | bytes 307216 | tf_op jit(solution)/shard_map/psum | solution.py:68
  1018.5 1.6 copy.47
  1020.1 1.6 copy.48
  (37 shorter events, 4.9 us)
Async XLA Ops:
  7.2 109.3 %copy-start = (bf16[1,16,128,128]{3,2,1,0:T(8,128)(2,1)S(1)}, bf16[1,16,128,128]{3,2,1,0:T(8,128)(2,1)}, u32[]{:S(2)}) copy-start(bf16[1,16,128,128]{3,2,1,0:T(8,128)(2,1)} %param.10) | copy-start | bytes 1572868
  7.2 107.4 %all-gather.3.cloned.1.call-start = ((), (), s32[]{:S(2)}) async-start(), calls=%async_computation.3 | async-start | bytes 1064960 | tf_op jit(solution)/shard_map/all_gather | solution.py:39
  9.5 170.2 %reduce-scatter.6.cloned.1.call-start = ((), (), s32[]{:S(2)}) async-start(), calls=%async_computation.4 | async-start | bytes 557056 | tf_op jit(solution)/shard_map/reduce_scatter | solution.py:43
  117.5 62.2 %copy-start.4 = (bf16[128,256]{1,0:T(8,128)(2,1)S(1)}, bf16[128,256]{1,0:T(8,128)(2,1)}, u32[]{:S(2)}) copy-start(bf16[128,256]{1,0:T(8,128)(2,1)} %param.13) | copy-start | bytes 196612
  117.5 63.8 %copy-start.1 = (bf16[1024,172]{0,1:T(8,128)(2,1)S(1)}, bf16[1024,172]{0,1:T(8,128)(2,1)}, u32[]{:S(2)}) copy-start(bf16[1024,172]{0,1:T(8,128)(2,1)} %param.15) | copy-start | bytes 1056772
  119.0 167.8 %all-gather.5.cloned.1.call-start = ((), (), s32[]{:S(2)}) async-start(), calls=%async_computation.5 | async-start | bytes 2129920 | tf_op jit(solution)/shard_map/all_gather | solution.py:39
  181.3 273.4 %reduce-scatter.10.cloned.1.call-start = ((), (), s32[]{:S(2)}) async-start(), calls=%async_computation.7 | async-start | bytes 4259840
  188.7 337.4 %reduce-scatter.8.cloned.1.call-start = ((), (), s32[]{:S(2)}) async-start(), calls=%async_computation.6 | async-start | bytes 1114112 | tf_op jit(solution)/shard_map/reduce_scatter | solution.py:43
  296.6 158.1 %copy-start.2 = (bf16[256,172]{0,1:T(8,128)(2,1)S(1)}, bf16[256,172]{0,1:T(8,128)(2,1)}, u32[]{:S(2)}) copy-start(bf16[256,172]{0,1:T(8,128)(2,1)} %param.14) | copy-start | bytes 264196
  296.6 159.1 %copy-start.3 = (f32[64,128]{1,0:T(8,128)S(1)}, f32[64,128]{1,0:T(8,128)}, u32[]{:S(2)}) copy-start(f32[64,128]{1,0:T(8,128)} %reduce-scatter.6.cloned.1.call-done) | copy-start | bytes 98308
  297.9 720.6 %all-reduce.3.cloned.1.call-start = ((), (), s32[]{:S(2)}) async-start(), calls=%async_computation.8 | async-start | bytes 622592 | tf_op jit(solution)/shard_map/psum | solution.py:68
Sparse Core Ops, SparseCore 0:
  13.1 101.3 all-gather.2
  119.2 60.4 reduce-scatter.5
  185.6 101.2 all-gather.4
  293.6 161.0 reduce-scatter.9
  457.9 68.2 reduce-scatter.7
  533.2 485.2 all-reduce.2
where the time goes:
time: 1030 us
  waiting for transfers between devices  977 us (95%)
  local copies, waits for them, and re-layouts  17.3 us (2%)
  matrix products  15.6 us (2%)
  between operations  14.9 us (1%)
    psum x1, waiting for transfers between devices, shards(): lax.psum((grad_first, grad_second), ('row', 'col'))  489 us
    all_gather x2, waiting for transfers between devices, aggregate(): gathered = lax.all_gather(source, 'row', axis=0, tiled=True)  201 us
    unnamed x7, waiting for transfers between devices  157 us
    reduce_scatter x2, waiting for transfers between devices, aggregate(): lax.psum_scatter(partial_rows.reshape(tile_rows * 128, width), 'col', sca...  130 us
  transfers between devices with their start and end apart: 6, of which 6 were waited for; matrix products, arithmetic and copies ran while one was open for 2% of the time, Pallas kernels for 0%

commit v1 on v0

v1 whole, which is shorter than its diff:
```python
import functools

import jax
import jax.numpy as jnp
from jax import lax
from jax.experimental import pallas as pl
from jax.experimental.pallas import tpu as pltpu
from jax.sharding import PartitionSpec as P

MESH = pl.DeviceIdType.MESH
F32, BF16 = jnp.float32, jnp.bfloat16
CURVE = 0.7978845608028654
CUBIC = 0.044715


def dot(left, right, contract=((1,), (0,))):
    return lax.dot_general(left, right, (contract, ((), ())), preferred_element_type=F32)


def split(value):
    high = value.astype(BF16)
    return high, (value - high.astype(F32)).astype(BF16)


def kernel(
    dims, feat, deg, tiles_hbm, table, w1, w2, cot_hbm, logits, out_first, out_second,
    tiles, flipped, forward, backward, cot, scot, scale, w2p,
    g1, g2, p1, r1, p2, r2, terms, sib, tsum, tx, ty,
    grad, gsib, gx, gsum, gy, gz, gfull,
    local_sem, send_sem, g1y, g1x, g1s, g2y, g2x, g2s, one_sem,
):
    nx, ny, nz = dims
    row, z = lax.axis_index("row"), lax.axis_index("col")
    core = lax.rem(row, 2)
    chip = row // 2
    x, y = lax.rem(chip, nx), chip // nx
    other = 1 - core
    node_rows, cls = logits.shape
    width = scot.shape[1]
    stripe = nz * node_rows
    slots = tiles_hbm.shape[0]

    def device(yy, xx, kk):
        return (yy * nx + xx) * 2 + kk, z

    def send(src, dst, to, send_id, recv):
        pltpu.make_async_remote_copy(
            src_ref=src, dst_ref=dst, send_sem=send_sem.at[send_id], recv_sem=recv,
            device_id=to, device_id_type=MESH,
        ).start()

    def await_bytes(ref, sem):
        pltpu.make_async_copy(ref, ref, sem).wait()

    tiles_copy = pltpu.make_async_copy(tiles_hbm, tiles.at[pl.ds(0, slots)], local_sem.at[0])
    tiles_copy.start()
    cot_copy = pltpu.make_async_copy(cot_hbm, cot, local_sem.at[1])
    cot_copy.start()

    barrier = pltpu.get_barrier_semaphore()

    def greet(to):
        pl.semaphore_signal(barrier, inc=1, device_id=to, device_id_type=MESH)

    for step in range(1, ny):
        greet(device(lax.rem(y + step, ny), x, core))
    for step in range(1, nx):
        greet(device(y, lax.rem(x + step, nx), core))
    greet(device(y, x, other))

    @pl.loop(1, nz)
    def _(step):
        greet((row, lax.rem(z + step, nz)))

    for block in range(stripe // 128):
        line = lax.rsqrt(deg[block:block + 1, :].astype(F32))
        scale[block * 128:(block + 1) * 128, :] = jnp.broadcast_to(line, (128, 128)).T
    own = scale[pl.ds(pl.multiple_of(z * node_rows, node_rows), node_rows), :]
    own_wide = jnp.concatenate([own] * (width // 128), axis=1)
    g1[y, x, core] = (own * feat[...].astype(F32)).astype(BF16)

    pl.semaphore_wait(barrier, (ny - 1) + (nx - 1) + 1 + (nz - 1))

    y_order = sorted(range(1, ny), key=lambda step: min(step, ny - step))

    def gather_start(g, ysem, xsem, ids):
        for step in y_order:
            mine = g.at[y, x, core]
            send(mine, mine, device(lax.rem(y + step, ny), x, core), ids, ysem.at[y])
        for step in range(1, nx):
            mine = g.at[y, x, core]
            send(mine, mine, device(y, lax.rem(x + step, nx), core), ids + 1, xsem.at[x])

    def gather_rows(g, ysem, xsem, ssem, ids):
        for step in y_order:
            yy = lax.rem(y + step, ny)
            block = g.at[yy, x, core]
            await_bytes(block, ysem.at[yy])
            for side in range(1, nx):
                send(block, block, device(y, lax.rem(x + side, nx), core), ids + 1, xsem.at[x])
        column = g.at[:, x, core]
        send(column, column, device(y, x, other), ids + 2, ssem.at[x])

    def gather_columns(g, xsem, ssem, ids):
        for side in range(1, nx):
            xx = lax.rem(x + side, nx)
            column = g.at[:, xx, core]
            await_bytes(column, xsem.at[xx])
            send(column, column, device(y, x, other), ids + 2, ssem.at[xx])

    def gather_finish(g, ssem):
        for xx in range(nx):
            await_bytes(g.at[:, xx, other], ssem.at[xx])

    def gather_sent(g, ids):
        await_bytes(g.at[pl.ds(0, ny - 1), 0, 0], send_sem.at[ids])
        await_bytes(g.at[:, pl.ds(0, nx - 1), 0], send_sem.at[ids + 1])
        await_bytes(g.at[:, :, 0], send_sem.at[ids + 2])

    def aggregate(g, p, r, ids, sem):
        total = ny * nx * 2 * node_rows
        span = min(256, stripe)
        peers = span // node_rows

        @pl.loop(0, stripe // span)
        def _(part):
            rows = forward[pl.ds(pl.multiple_of(part * span, span), span), :]
            value = dot(rows, g[...].reshape(total, g.shape[-1])).astype(BF16)
            p[pl.ds(part * peers, peers)] = value.reshape(peers, node_rows, g.shape[-1])
            for peer in range(peers):
                to = part * peers + peer

                @pl.when(to != z)
                def _():
                    send(p.at[to], r.at[z], (row, to), ids, sem)

        r[z] = p[z]

    def aggregate_sum(r, sem):
        await_bytes(r.at[pl.ds(0, nz - 1)], sem)
        return functools.reduce(lambda a, b: a + b, [r[i].astype(F32) for i in range(nz)])

    gather_start(g1, g1y, g1x, 0)

    tiles_copy.wait()
    tiles[slots] = jnp.zeros((128, 128), BF16)
    tile_rows, tile_cols = stripe // 128, ny * nx

    @pl.loop(0, tile_cols)
    def _(c):
        for r in range(tile_rows):
            forward[r * 128:(r + 1) * 128, pl.ds(pl.multiple_of(c * 128, 128), 128)] = tiles[
                table[r * tile_cols + c]
            ]

    gather_rows(g1, g1y, g1x, g1s, 0)

    @pl.loop(0, slots + 1)
    def _(t):
        flipped[t] = tiles[t].astype(F32).T.astype(BF16)

    @pl.loop(0, tile_cols)
    def _(c):
        for r in range(tile_rows):
            backward[pl.ds(pl.multiple_of(c * 128, 128), 128), r * 128:(r + 1) * 128] = flipped[
                table[r * tile_cols + c]
            ]

    cot_copy.wait()
    scot[:, 128:] = jnp.zeros((stripe, width - 128), BF16)

    @pl.loop(0, tile_rows)
    def _(r):
        rows = pl.ds(pl.multiple_of(r * 128, 128), 128)
        value, by = cot[rows, :].astype(F32), scale[rows, :]
        scot[rows, :128] = (value[:, :128] * by).astype(BF16)
        scot[rows, 128:cls] = (value[:, 128:] * by[:, :cls - 128]).astype(BF16)

    w2p[:, 128:] = jnp.zeros((w2p.shape[0], width - 128), BF16)
    w2p[:, :cls] = w2[...]

    @pl.loop(0, ny)
    def _(line):
        rows = backward[pl.ds(pl.multiple_of(line * nx * 128, nx * 128), nx * 128), :]
        value = dot(rows, scot[...]).astype(BF16)
        terms[line] = value.reshape(nx, 2, node_rows, width)
        send(terms.at[line, :, other], sib.at[line], device(y, x, other), 6, one_sem.at[0])

    gather_columns(g1, g1x, g1s, 0)
    gather_finish(g1, g1s)
    aggregate(g1, p1, r1, 7, one_sem.at[1])

    await_bytes(sib, one_sem.at[0])

    @pl.loop(0, ny)
    def _(line):
        for xx in range(nx):
            tsum[xx, line] = (
                terms[line, xx, core].astype(F32) + sib[line, xx].astype(F32)
            ).astype(BF16)

    for side in range(1, nx):
        xx = lax.rem(x + side, nx)
        send(tsum.at[xx], tx.at[x], device(y, xx, core), 8, one_sem.at[2])
    tx[x] = tsum[x]

    first_agg = (own * aggregate_sum(r1, one_sem.at[1])).astype(BF16)
    first_pre = dot(first_agg, w1[...])
    bend = jnp.tanh(CURVE * (first_pre + CUBIC * first_pre * first_pre * first_pre))
    hidden = (own_wide * (0.5 * first_pre * (1.0 + bend))).astype(BF16)
    slope = 0.5 * (1.0 + bend) + 0.5 * first_pre * (1.0 - bend * bend) * (
        CURVE * (1.0 + 3.0 * CUBIC * first_pre * first_pre)
    )
    g2[y, x, core] = dot(hidden, w2p[...]).astype(BF16)
    gather_start(g2, g2y, g2x, 3)

    await_bytes(tx.at[pl.ds(0, nx - 1)], one_sem.at[2])

    @pl.loop(0, ny)
    def _(line):
        value = functools.reduce(lambda a, b: a + b, [tx[i, line].astype(F32) for i in range(nx)])
        tsum[x, line] = value.astype(BF16)

    for step in range(1, ny):
        yy = lax.rem(y + step, ny)
        send(tsum.at[x, yy], ty.at[y], device(yy, x, core), 9, one_sem.at[3])
    ty[y] = tsum[x, y]

    gather_rows(g2, g2y, g2x, g2s, 3)

    await_bytes(ty.at[pl.ds(0, ny - 1)], one_sem.at[3])
    narrow = functools.reduce(lambda a, b: a + b, [ty[i].astype(F32) for i in range(ny)])
    high, low = split(narrow)
    back = dot(high, w2p[...], ((1,), (1,))) + dot(low, w2p[...], ((1,), (1,)))
    grad_pre = (own_wide * back * slope).astype(BF16)
    first_rows = dot(first_agg, grad_pre, ((0,), (0,)))
    second_rows = dot(hidden, high, ((0,), (0,))) + dot(hidden, low, ((0,), (0,)))
    n_first, n_second = first_rows.shape[0], second_rows.shape[0]
    chunk = grad.shape[3]
    spare = 2 * nx * ny * chunk - n_first - n_second
    grad[...] = jnp.concatenate(
        [first_rows, second_rows, jnp.zeros((spare, width), F32)], axis=0
    ).reshape(grad.shape)
    send(grad.at[other], gsib, device(y, x, other), 10, one_sem.at[4])

    gather_columns(g2, g2x, g2s, 3)

    await_bytes(gsib, one_sem.at[4])
    gsib[...] = gsib[...] + grad[core]
    for side in range(1, nx):
        xx = lax.rem(x + side, nx)
        send(gsib.at[xx], gx.at[x], device(y, xx, core), 11, one_sem.at[5])
    gx[x] = gsib[x]

    gather_finish(g2, g2s)
    aggregate(g2, p2, r2, 12, one_sem.at[6])

    await_bytes(gx.at[pl.ds(0, nx - 1)], one_sem.at[5])
    gsum[...] = functools.reduce(lambda a, b: a + b, [gx[i] for i in range(nx)])
    for step in range(1, ny):
        yy = lax.rem(y + step, ny)
        send(gsum.at[yy], gy.at[y], device(yy, x, core), 13, one_sem.at[7])
    gy[y] = gsum[y]
    await_bytes(gy.at[pl.ds(0, ny - 1)], one_sem.at[7])
    gz[z] = functools.reduce(lambda a, b: a + b, [gy[i] for i in range(ny)])

    @pl.loop(1, nz)
    def _(step):
        send(gz.at[z], gz.at[z], (row, lax.rem(z + step, nz)), 14, one_sem.at[8])

    await_bytes(gz.at[pl.ds(0, nz - 1)], one_sem.at[8])
    gfull[core, x, y] = functools.reduce(lambda a, b: a + b, [gz[i] for i in range(nz)])
    mine = gfull.at[core, x, y]
    for step in range(1, ny):
        send(mine, mine, device(lax.rem(y + step, ny), x, core), 15, one_sem.at[9])
    await_bytes(gx.at[0, pl.ds(0, ny - 1)], one_sem.at[9])
    mine_x = gfull.at[core, x]
    for side in range(1, nx):
        send(mine_x, mine_x, device(y, lax.rem(x + side, nx), core), 16, one_sem.at[10])
    await_bytes(gx.at[pl.ds(0, nx - 1)], one_sem.at[10])
    send(gfull.at[core], gfull.at[core], device(y, x, other), 17, one_sem.at[11])

    second = own_wide * aggregate_sum(r2, one_sem.at[6])
    logits[...] = second[:, :cls].astype(BF16)

    await_bytes(gsib, one_sem.at[11])
    whole = gfull[...].reshape(2 * nx * ny * chunk, width)
    out_first[...] = whole[:n_first]
    out_second[...] = whole[n_first:n_first + n_second, :cls]

    gather_sent(g1, 0)
    gather_sent(g2, 3)
    await_bytes(sib, send_sem.at[6])
    await_bytes(r1.at[pl.ds(0, nz - 1)], send_sem.at[7])
    await_bytes(tx.at[pl.ds(0, nx - 1)], send_sem.at[8])
    await_bytes(ty.at[pl.ds(0, ny - 1)], send_sem.at[9])
    await_bytes(gsib, send_sem.at[10])
    await_bytes(gx.at[pl.ds(0, nx - 1)], send_sem.at[11])
    await_bytes(r2.at[pl.ds(0, nz - 1)], send_sem.at[12])
    await_bytes(gy.at[pl.ds(0, ny - 1)], send_sem.at[13])
    await_bytes(gz.at[pl.ds(0, nz - 1)], send_sem.at[14])
    await_bytes(gx.at[0, pl.ds(0, ny - 1)], send_sem.at[15])
    await_bytes(gx.at[pl.ds(0, nx - 1)], send_sem.at[16])
    await_bytes(gsib, send_sem.at[17])


def shards(dims, features, degrees, tiles, tile_slots, tile_counts, w_first, w_second, cotangent):
    nx, ny, nz = dims
    node_rows, f_in = features.shape
    slots = tiles.shape[1]
    hid, cls = w_second.shape
    stripe = nz * node_rows
    tile_rows, tile_cols = stripe // 128, ny * nx
    width = 256
    chunk = 512 // (2 * nx * ny)
    cells = jnp.arange(tile_rows * tile_cols, dtype=jnp.int32)
    order = jnp.arange(slots, dtype=jnp.int32)
    hit = (tile_slots[0][None, :] == cells[:, None]) & (order < tile_counts[0])[None, :]
    table = jnp.sum(jnp.where(hit, order - slots, 0), axis=1, dtype=jnp.int32) + slots
    vmem = pl.BlockSpec(memory_space=pltpu.VMEM)
    far = pl.BlockSpec(memory_space=pl.ANY)
    scratch = lambda *shape, dtype=BF16: pltpu.VMEM(shape, dtype)
    sems = lambda n: pltpu.SemaphoreType.DMA((n,))
    return pl.pallas_call(
        functools.partial(kernel, dims),
        out_shape=(
            jax.ShapeDtypeStruct((node_rows, cls), BF16),
            jax.ShapeDtypeStruct((f_in, hid), F32),
            jax.ShapeDtypeStruct((hid, cls), F32),
        ),
        in_specs=[vmem, vmem, far, pl.BlockSpec(memory_space=pltpu.SMEM), vmem, vmem, far],
        out_specs=(vmem, vmem, vmem),
        scratch_shapes=[
            scratch(slots + 1, 128, 128),
            scratch(slots + 1, 128, 128),
            scratch(stripe, tile_cols * 128),
            scratch(tile_cols * 128, stripe),
            scratch(stripe, cls),
            scratch(stripe, width),
            scratch(stripe, 128, dtype=F32),
            scratch(hid, width),
            scratch(ny, nx, 2, node_rows, f_in),
            scratch(ny, nx, 2, node_rows, width),
            scratch(nz, node_rows, f_in),
            scratch(nz, node_rows, f_in),
            scratch(nz, node_rows, width),
            scratch(nz, node_rows, width),
            scratch(ny, nx, 2, node_rows, width),
            scratch(ny, nx, node_rows, width),
            scratch(nx, ny, node_rows, width),
            scratch(nx, ny, node_rows, width),
            scratch(ny, node_rows, width),
            scratch(2, nx, ny, chunk, width, dtype=F32),
            scratch(nx, ny, chunk, width, dtype=F32),
            scratch(nx, ny, chunk, width, dtype=F32),
            scratch(ny, chunk, width, dtype=F32),
            scratch(ny, chunk, width, dtype=F32),
            scratch(nz, chunk, width, dtype=F32),
            scratch(2, nx, ny, chunk, width, dtype=F32),
            sems(2),
            sems(18),
            sems(ny), sems(nx), sems(nx),
            sems(ny), sems(nx), sems(nx),
            sems(12),
        ],
        compiler_params=pltpu.CompilerParams(
            collective_id=0, has_side_effects=True, vmem_limit_bytes=48 * 1024 * 1024
        ),
    )(
        features, degrees.reshape(tile_rows, 128), tiles[0], table, w_first, w_second, cotangent
    )


def solution(mesh):
    ny = 8 if mesh.shape["row"] == 64 else 2
    dims = (mesh.shape["row"] // (2 * ny), ny, mesh.shape["col"])
    placed = (
        P(("row", "col"), None),
        P("row"),
        P(("row", "col"), None, None, None),
        P(("row", "col"), None),
        P(("row", "col")),
        P(),
        P(),
        P("row", None),
    )
    return jax.shard_map(
        functools.partial(shards, dims),
        mesh=mesh,
        in_specs=placed,
        out_specs=(P(("row", "col"), None), P(), P()),
        check_vma=False,
    )
```

time: 1030 us -> 124 us (0.12)
  waiting for transfers between devices: 977 us -> 0 us
  Pallas kernels: 0 us -> 118 us
  matrix products: 15.6 us -> 0 us
  between operations: 14.9 us -> 1.38 us
  local copies, waits for them, and re-layouts: 17.3 us -> 4.97 us
    psum x1 -> x0, waiting for transfers between devices: 489 us -> none  [shards(): lax.psum((grad_first, grad_second), ('row', 'col'))]
    all_gather x2 -> x0, waiting for transfers between devices: 201 us -> none  [aggregate(): gathered = lax.all_gather(source, 'row', axis=0, tiled=True)]
    unnamed x7 -> x0, waiting for transfers between devices: 157 us -> none
    reduce_scatter x2 -> x0, waiting for transfers between devices: 130 us -> none  [aggregate(): lax.psum_scatter(partial_rows.reshape(tile_rows * 128, width), 'col', sca...]
    pallas_call x0 -> x1, Pallas kernels: none -> 118 us  [shards(): pl.pallas_call(functools.partial(kernel, dims), out_shape=(jax.ShapeDtype...]
    dot_general x11 -> x0, matrix products: 15.6 us -> none  [the longest x2 3.32 us: aggregate(): jnp.einsum('rt,tif->rif', row_pick, prods, precision=lax.Precision.HIGHEST)]
  transfers between devices with their start and end apart: 6 -> 0, of which waited for: 6 -> 0; matrix products, arithmetic and copies ran while one was open for 2% -> 0% of each run, Pallas kernels for 0% -> 0%
where the time goes in v1:
time: 124 us
  Pallas kernels  118 us (95%)
  local copies, waits for them, and re-layouts  4.97 us (4%)
  between operations  1.38 us (1%)
    pallas_call x1, Pallas kernels, shards(): pl.pallas_call(functools.partial(kernel, dims), out_shape=(jax.ShapeDtype...  118 us
    unnamed x14, local copies, waits for them, and re-layouts  4.18 us

profile of v1, /device:TPU:1, one launch (start us, length us, event | category | flops | bytes accessed | tf_op | source)
XLA Modules:
  0.0 124.0 jit_solution(6114423408353827795)
XLA Ops:
  1.3 0.0 copy-start.4
  1.3 0.6 copy-done.4
  1.9 0.1 select_reduce_fusion
  2.0 0.0 copy-start
  2.1 1.0 copy.14.w2
  3.1 0.0 copy-start.1
  3.1 0.0 copy-start.2
  3.1 0.0 copy-start.3
  3.1 1.2 copy.15.cot_hbm
  4.4 0.0 copy-done
  4.4 0.0 copy-done.1
  4.4 0.0 copy-done.2
  4.4 0.0 copy-done.3
  4.4 117.5 %shard_map.103 = (bf16[64,172]{1,0:T(8,128)(2,1)S(1)}, f32[128,256]{1,0:T(8,128)S(1)}, f32[256,172]{1,0:T(8,128)S(1)}) custom-call(bf16[64,128]{1,0:T(8,128)(2,1)S(1)} %copy-done.2, s32[8,128]{1,0:T(8,128)S(1)} %bitcast.6, bf16[16,128,128]{2,1,0:T(8,128)(2,1)S(1)} %bitcast.5, s32[256]{0:T(256)S(1)} %broadcast_add_fusion.table, ...), custom_call_target="tpu_custom_call" | custom-call | tf_op jit(solution)/shard_map/pallas_call | solution.py:324
  121.9 0.8 copy.16
  122.7 0.6 copy.20
  123.3 0.7 copy.21
  (3 shorter events, 0.0 us)
Async XLA Ops:
  1.3 0.7 copy-start.4
  2.0 2.3 %copy-start = (bf16[1,16,128,128]{3,2,1,0:T(8,128)(2,1)S(1)}, bf16[1,16,128,128]{3,2,1,0:T(8,128)(2,1)}, u32[]{:S(2)}) copy-start(bf16[1,16,128,128]{3,2,1,0:T(8,128)(2,1)} %param.10) | copy-start | bytes 1572868
  3.1 1.3 %copy-start.1 = (bf16[128,256]{1,0:T(8,128)(2,1)S(1)}, bf16[128,256]{1,0:T(8,128)(2,1)}, u32[]{:S(2)}) copy-start(bf16[128,256]{1,0:T(8,128)(2,1)} %w1.1) | copy-start | bytes 196612
  3.1 1.3 %copy-start.2 = (bf16[64,128]{1,0:T(8,128)(2,1)S(1)}, bf16[64,128]{1,0:T(8,128)(2,1)}, u32[]{:S(2)}) copy-start(bf16[64,128]{1,0:T(8,128)(2,1)} %feat.1) | copy-start | bytes 49156
  3.1 1.3 %copy-start.3 = (s32[1024]{0:T(1024)S(1)}, s32[1024]{0:T(1024)}, u32[]{:S(2)}) copy-start(s32[1024]{0:T(1024)} %param.9) | copy-start | bytes 12292

commit v2 on v1

v2 whole, which is shorter than its diff:
```python
import functools

import jax
import jax.numpy as jnp
from jax import lax
from jax.experimental import pallas as pl
from jax.experimental.pallas import tpu as pltpu
from jax.sharding import PartitionSpec as P

MESH = pl.DeviceIdType.MESH
F32, BF16 = jnp.float32, jnp.bfloat16
CURVE = 0.7978845608028654
CUBIC = 0.044715
HALF = 96


def dot(left, right, contract=((1,), (0,))):
    return lax.dot_general(left, right, (contract, ((), ())), preferred_element_type=F32)


def split(value):
    high = value.astype(BF16)
    return high, (value - high.astype(F32)).astype(BF16)


def total(parts):
    parts = list(parts)
    while len(parts) > 1:
        parts = [a + b for a, b in zip(parts[::2], parts[1::2])] + parts[len(parts) & ~1:]
    return parts[0]


def kernel(
    dims, feat, deg, tiles_hbm, table, w1, w2t, cot_hbm, logits, out_first, out_second,
    tiles, adjacency, cot, scot, w2p, turned, own_scale,
    g1, g2, source, p1, r1, q1, p2, r2, q2, terms, sib, tsum, tx, ty, narrow_t, back_all,
    grad, gsib, gys, gy, gxs, gx, gz, gfull,
    local_sem, send_sem, g1y, g1x, g1s, g2y, g2x, g2s, one_sem,
):
    nx, ny, nz = dims
    row, z = lax.axis_index("row"), lax.axis_index("col")
    core = lax.rem(row, 2)
    chip = row // 2
    x, y = lax.rem(chip, nx), chip // nx
    other = 1 - core
    node_rows, cls = logits.shape
    stripe = nz * node_rows
    slots = tiles_hbm.shape[0]
    tile_rows, tile_cols = stripe // 128, ny * nx
    finish = []

    def device(yy, xx, kk):
        return (yy * nx + xx) * 2 + kk, z

    def send(src, dst, to, send_id, recv):
        pltpu.make_async_remote_copy(
            src_ref=src, dst_ref=dst, send_sem=send_sem.at[send_id], recv_sem=recv,
            device_id=to, device_id_type=MESH,
        ).start()

    def await_bytes(ref, sem):
        if 0 in ref.shape:
            return
        pltpu.make_async_copy(ref, ref, sem).wait()

    def sent(ref, send_id, some=1):
        if some:
            finish.append(lambda: await_bytes(ref, send_sem.at[send_id]))

    tiles_copy = pltpu.make_async_copy(tiles_hbm, tiles.at[pl.ds(0, slots)], local_sem.at[0])
    tiles_copy.start()
    cot_copy = pltpu.make_async_copy(cot_hbm, cot, local_sem.at[1])
    cot_copy.start()

    barrier = pltpu.get_barrier_semaphore()

    def greet(to):
        pl.semaphore_signal(barrier, inc=1, device_id=to, device_id_type=MESH)

    for step in range(1, ny):
        greet(device(lax.rem(y + step, ny), x, core))
    for step in range(1, nx):
        greet(device(y, lax.rem(x + step, nx), core))
    greet(device(y, x, other))

    @pl.loop(1, nz)
    def _(step):
        greet((row, lax.rem(z + step, nz)))

    per_line = 128 // node_rows
    line = lax.rsqrt(deg[pl.ds(z // per_line, 1), :].astype(F32))
    own_scale[...] = jnp.broadcast_to(line, (128, 128)).T
    own = own_scale[pl.ds(pl.multiple_of(lax.rem(z, per_line) * node_rows, node_rows), node_rows), :]
    own_wide = jnp.concatenate([own, own], axis=1)
    g1[y, x, core] = (own * feat[...].astype(F32)).astype(BF16)

    pl.semaphore_wait(barrier, (ny - 1) + (nx - 1) + 1 + (nz - 1))

    y_order = sorted(range(1, ny), key=lambda step: min(step, ny - step))

    pairs = ny // 2

    def gather_start(g, ysem, xsem, ids):
        mine = g.at[y, x, core]
        for step in y_order:
            send(mine, mine, device(lax.rem(y + step, ny), x, core), ids, ysem.at[y])
        for step in range(1, nx):
            to = device(y, lax.rem(x + step, nx), core)
            send(mine, mine, to, ids + 1, xsem.at[x, y // 2])
        sent(g.at[pl.ds(0, ny - 1), 0, 0], ids)
        sent(g.at[:, pl.ds(0, nx - 1), 0], ids + 1, nx - 1)
        sent(g.at[:, :, 0], ids + 2)

    def gather_rows(g, ysem, xsem, ssem, ids):
        for step in y_order:
            yy = lax.rem(y + step, ny)
            block = g.at[yy, x, core]
            await_bytes(block, ysem.at[yy])
            for side in range(1, nx):
                to = device(y, lax.rem(x + side, nx), core)
                send(block, block, to, ids + 1, xsem.at[x, yy // 2])
        column = g.at[:, x, core]
        send(column, column, device(y, x, other), ids + 2, ssem.at[x])

    def gather_columns(g, xsem, ssem, ids, steps):
        for step in steps:
            pair = lax.rem(y // 2 + step, pairs)
            for side in range(1, nx):
                xx = lax.rem(x + side, nx)
                blocks = g.at[pl.ds(pair * 2, 2), xx, core]
                await_bytes(blocks, xsem.at[xx, pair])
                send(blocks, blocks, device(y, x, other), ids + 2, ssem.at[xx])

    pair_order = sorted(range(pairs), key=lambda step: min(step, pairs - step))

    def gather_finish(g, ssem):
        for xx in range(nx):
            await_bytes(g.at[:, xx, other], ssem.at[xx])

    reach = nz // 4

    def aggregate(source_of, pack, p, r, ids, sem, far_sem):
        span = min(256, stripe)
        peers, parts = span // node_rows, stripe // span
        half = p.shape[1] // 2

        @pl.loop(0, parts)
        def _(i):
            part = i
            if parts == 4:
                turn = (1 - i // 2) * (2 + i) + (i // 2) * (3 - i)
                part = lax.rem(z // peers + turn, parts)
            rows = adjacency[pl.ds(pl.multiple_of(part * span, span), span), :]
            value = dot(rows, source_of())
            for peer in range(peers):
                to = part * peers + peer
                p[to] = pack(value[peer * node_rows:(peer + 1) * node_rows])
                ahead = lax.rem(to - z + nz, nz)

                if reach > 1:
                    @pl.when(lax.rem(ahead, reach) != 0)
                    def _():
                        side = 1 - ahead // (nz // 2)
                        away = side * ahead + (1 - side) * (nz - ahead)
                        far = (away - 1) // reach
                        hop = away - reach * far
                        slot = far * (2 * reach + side * (reach - 1)) + (1 - far) * side * reach + hop - 1
                        target = lax.rem(z + (2 * side - 1) * hop + nz, nz)
                        send(p.at[to], r.at[slot], (row, target), ids, one_sem.at[sem + far * (far_sem - sem)])

                @pl.when(ahead == nz // 2)
                def _():
                    for side in range(2):
                        rows = pl.ds(side * half, half)
                        target = lax.rem(z + (2 * side - 1) * reach + nz, nz)
                        send(p.at[to, rows], r.at[4 * reach - 2, rows], (row, target), ids, one_sem.at[far_sem])

        r[4 * reach - 1] = p[z]
        sent(r.at[pl.ds(0, nz - 1)], ids)

    def relay(p, r, q, ids, sem, far_sem):
        half = p.shape[1] // 2
        await_bytes(r.at[pl.ds(2 * reach, 2 * reach - 1)], one_sem.at[far_sem])
        opposite = r[4 * reach - 2].astype(F32)
        nothing = jnp.zeros((half, 128), F32)
        for side in range(2):
            to = lax.rem(z + (2 * side - 1) * reach + nz, nz)
            first = 2 * reach + side * (reach - 1)
            part = (
                jnp.concatenate([nothing, opposite[half:]], axis=0) if side
                else jnp.concatenate([opposite[:half], nothing], axis=0)
            )
            value = total([part, p[to].astype(F32)] + [r[first + i].astype(F32) for i in range(reach - 1)])
            q[side] = value.astype(BF16)
            send(q.at[side], r.at[side * reach + reach - 1], (row, to), ids, one_sem.at[sem])

    def aggregate_sum(r, sem):
        await_bytes(r.at[pl.ds(0, 2 * reach)], one_sem.at[sem])
        return total(r[i].astype(F32) for i in list(range(2 * reach)) + [4 * reach - 1])

    short = node_rows // 2
    low_lanes = lax.broadcasted_iota(jnp.int32, (short, 128), 1) < 64

    def pack_classes(value):
        first, second = value[:short, 128:], pltpu.roll(value[short:, 128:], 64, 1)
        tail = jnp.where(low_lanes, first, second)
        return jnp.concatenate([value[:, :128], tail], axis=0).astype(BF16)

    def finish_all():
        for wait in finish:
            wait()


    gather_start(g1, g1y, g1x, 0)

    tiles_copy.wait()
    tiles[slots] = jnp.zeros((128, 128), BF16)

    @pl.loop(0, tile_cols)
    def _(c):
        for r in range(tile_rows):
            adjacency[r * 128:(r + 1) * 128, pl.ds(pl.multiple_of(c * 128, 128), 128)] = tiles[
                table[r * tile_cols + c]
            ]

    gather_rows(g1, g1y, g1x, g1s, 0)

    cot_copy.wait()
    scot[cls // 16 * 16:, :] = jnp.zeros((2 * HALF - cls // 16 * 16, stripe), BF16)
    for r in range(tile_rows):
        by = lax.rsqrt(deg[r:r + 1, :].astype(F32))
        scot[:cls, r * 128:(r + 1) * 128] = (
            cot[:, r * 128:(r + 1) * 128].astype(F32) * by
        ).astype(BF16)
    w2p[cls // 16 * 16:, :] = jnp.zeros((w2p.shape[0] - cls // 16 * 16, w2p.shape[1]), BF16)
    w2p[:cls, :] = w2t[...]

    @pl.loop(0, ny)
    def _(part):
        columns = pl.ds(pl.multiple_of(part * nx * 128, nx * 128), nx * 128)
        value = dot(scot[...], adjacency[:, columns]).astype(BF16)
        for xx in range(nx):
            terms[part, xx] = value[:, xx * 128:(xx + 1) * 128].reshape(2, HALF, 128)
        send(terms.at[part, :, other], sib.at[part], device(y, x, other), 6, one_sem.at[0])

    sent(sib, 6)

    gather_columns(g1, g1x, g1s, 0, pair_order)

    await_bytes(sib, one_sem.at[0])

    @pl.loop(0, ny)
    def _(part):
        for xx in range(nx):
            tsum[xx, part] = (
                terms[part, xx, core].astype(F32) + sib[part, xx].astype(F32)
            ).astype(BF16)

    for side in range(1, nx):
        xx = lax.rem(x + side, nx)
        send(tsum.at[xx], tx.at[x], device(y, xx, core), 8, one_sem.at[2])
    sent(tx.at[pl.ds(0, nx - 1)], 8, nx - 1)
    tx[x] = tsum[x]

    gather_finish(g1, g1s)
    nodes = tile_cols * 128
    aggregate(lambda: g1[...].reshape(nodes, 128), lambda v: v.astype(BF16), p1, r1, 7, 1, 13)
    relay(p1, r1, q1, 7, 1, 13)

    await_bytes(tx.at[pl.ds(0, nx - 1)], one_sem.at[2])

    @pl.loop(0, ny)
    def _(part):
        tsum[x, part] = total(tx[i, part].astype(F32) for i in range(nx)).astype(BF16)

    for step in y_order:
        yy = lax.rem(y + step, ny)
        send(tsum.at[x, yy], ty.at[y], device(yy, x, core), 9, one_sem.at[3])
    sent(ty.at[pl.ds(0, ny - 1)], 9)
    ty[y] = tsum[x, y]

    first_agg = (own * aggregate_sum(r1, 1)).astype(BF16)
    first_pre = dot(first_agg, w1[...])
    bend = jnp.tanh(CURVE * (first_pre + CUBIC * first_pre * first_pre * first_pre))
    hidden = (own_wide * (0.5 * first_pre * (1.0 + bend))).astype(BF16)
    g2[y, x, core] = pack_classes(dot(hidden, w2p[...], ((1,), (1,))))
    gather_start(g2, g2y, g2x, 3)

    slope = 0.5 * (1.0 + bend) + 0.5 * first_pre * (1.0 - bend * bend) * (
        CURVE * (1.0 + 3.0 * CUBIC * first_pre * first_pre)
    )

    await_bytes(ty.at[pl.ds(0, ny - 1)], one_sem.at[3])
    narrow_t[core] = total(ty[i].astype(F32) for i in range(ny))
    mine = narrow_t.at[core]
    send(mine, mine, device(y, x, other), 18, one_sem.at[12])
    sent(mine, 18)

    gather_rows(g2, g2y, g2x, g2s, 3)

    n_first, hid = out_first.shape
    await_bytes(narrow_t.at[0], one_sem.at[12])
    lane_core = lax.broadcasted_iota(jnp.int32, (2 * HALF, 128), 1) // node_rows
    narrow = jnp.where(lane_core == core, narrow_t[...].reshape(2 * HALF, 128), 0.0)
    high, low = split(narrow)
    w2_rows = w2p[:2 * HALF, :]
    back_all[...] = dot(high, w2_rows, ((0,), (0,))) + dot(low, w2_rows, ((0,), (0,)))
    back = back_all[pl.ds(pl.multiple_of(core * node_rows, node_rows), node_rows), :]
    grad_pre = (own_wide * back * slope).astype(BF16)
    first_rows = dot(first_agg, grad_pre, ((0,), (0,)))
    hidden_twice = jnp.concatenate([hidden, hidden], axis=0)
    second_rows = dot(high, hidden_twice) + dot(low, hidden_twice)
    chunk = gz.shape[1] // 2
    spare = 2 * nx * ny * chunk - n_first - 2 * HALF
    grad[...] = jnp.concatenate(
        [first_rows, second_rows, jnp.zeros((spare, hid), F32)], axis=0
    ).reshape(grad.shape)
    send(grad.at[other], gsib, device(y, x, other), 10, one_sem.at[4])
    sent(gsib, 10)

    gather_columns(g2, g2x, g2s, 3, pair_order[:1])

    await_bytes(gsib, one_sem.at[4])
    gys[...] = (gsib[...] + grad[core]).astype(BF16)
    for step in y_order:
        yy = lax.rem(y + step, ny)
        send(gys.at[yy], gy.at[y], device(yy, x, core), 11, one_sem.at[5])
    sent(gy.at[pl.ds(0, ny - 1)], 11)
    gy[y] = gys[y]

    gather_columns(g2, g2x, g2s, 3, pair_order[1:])

    await_bytes(gy.at[pl.ds(0, ny - 1)], one_sem.at[5])
    gxs[...] = total(gy[i].astype(F32) for i in range(ny)).reshape(nx, chunk, hid)
    for side in range(1, nx):
        xx = lax.rem(x + side, nx)
        send(gxs.at[xx], gx.at[x], device(y, xx, core), 13, one_sem.at[7])
    sent(gx.at[pl.ds(0, nx - 1)], 13, nx - 1)
    gx[x] = gxs[x]

    gather_finish(g2, g2s)

    @pl.loop(0, tile_cols)
    def _(i):
        for k in range(2):
            block = g2[i // nx, lax.rem(i, nx), k]
            tail = block[node_rows:].astype(F32)
            tail = jnp.concatenate([tail, pltpu.roll(tail, 64, 1)], axis=0).astype(BF16)
            rows = pl.ds(pl.multiple_of(i * 128 + k * node_rows, node_rows), node_rows)
            source[rows, :128] = block[:node_rows]
            source[rows, 128:] = tail

    await_bytes(gx.at[pl.ds(0, nx - 1)], one_sem.at[7])
    summed = total(gx[i] for i in range(nx))
    gz[z] = jnp.concatenate([summed[:, :128], summed[:, 128:]], axis=0).astype(BF16)

    @pl.loop(1, nz)
    def _(step):
        send(gz.at[z], gz.at[z], (row, lax.rem(z + step, nz)), 14, one_sem.at[8])

    sent(gz.at[pl.ds(0, nz - 1)], 14)

    aggregate(lambda: source[...], pack_classes, p2, r2, 12, 6, 14)
    relay(p2, r2, q2, 12, 6, 14)

    await_bytes(gz.at[pl.ds(0, nz - 1)], one_sem.at[8])
    summed = total(gz[i].astype(F32) for i in range(nz))
    gfull[core, y, x] = jnp.concatenate([summed[:chunk], summed[chunk:]], axis=1)
    mine_y = gfull.at[core, y, x]
    for step in y_order:
        send(mine_y, mine_y, device(lax.rem(y + step, ny), x, core), 15, one_sem.at[9])
    sent(gfull.at[0, pl.ds(0, ny - 1), 0], 15)
    await_bytes(gfull.at[0, pl.ds(0, ny - 1), 0], one_sem.at[9])
    mine_x = gfull.at[core, :, x]
    for side in range(1, nx):
        send(mine_x, mine_x, device(y, lax.rem(x + side, nx), core), 16, one_sem.at[10])
    sent(gfull.at[0, :, pl.ds(0, nx - 1)], 16, nx - 1)
    await_bytes(gfull.at[0, :, pl.ds(0, nx - 1)], one_sem.at[10])
    send(gfull.at[core], gfull.at[core], device(y, x, other), 17, one_sem.at[11])
    sent(gfull.at[0], 17)
    await_bytes(gfull.at[0], one_sem.at[11])
    whole = gfull[...].reshape(2 * nx * ny * chunk, hid)
    out_first[...] = whole[:n_first]
    out_second[...] = whole[n_first:n_first + cls]

    packed = aggregate_sum(r2, 6)
    tail = packed[node_rows:]
    tail = jnp.concatenate([tail, pltpu.roll(tail, 64, 1)], axis=0)
    logits[:, :128] = (own * packed[:node_rows]).astype(BF16)
    logits[:, 128:] = (own * tail)[:, :cls - 128].astype(BF16)

    finish_all()


def shards(dims, features, degrees, tiles, tile_slots, tile_counts, w_first, w_second, cotangent):
    nx, ny, nz = dims
    node_rows, f_in = features.shape
    slots = tiles.shape[1]
    hid, cls = w_second.shape
    stripe = nz * node_rows
    tile_rows, tile_cols = stripe // 128, ny * nx
    chunk = 512 // (2 * nx * ny)
    cells = jnp.arange(tile_rows * tile_cols, dtype=jnp.int32)
    order = jnp.arange(slots, dtype=jnp.int32)
    hit = (tile_slots[0][None, :] == cells[:, None]) & (order < tile_counts[0])[None, :]
    table = jnp.sum(jnp.where(hit, order - slots, 0), axis=1, dtype=jnp.int32) + slots
    vmem = pl.BlockSpec(memory_space=pltpu.VMEM)
    far = pl.BlockSpec(memory_space=pl.ANY)
    scratch = lambda *shape, dtype=BF16: pltpu.VMEM(shape, dtype)
    sems = lambda *shape: pltpu.SemaphoreType.DMA(shape)
    logits, grad_first, grad_second = pl.pallas_call(
        functools.partial(kernel, dims),
        out_shape=(
            jax.ShapeDtypeStruct((node_rows, cls), BF16),
            jax.ShapeDtypeStruct((f_in, hid), F32),
            jax.ShapeDtypeStruct((cls, hid), F32),
        ),
        in_specs=[vmem, vmem, far, pl.BlockSpec(memory_space=pltpu.SMEM), vmem, vmem, far],
        out_specs=(vmem, vmem, vmem),
        scratch_shapes=[
            scratch(slots + 1, 128, 128),
            scratch(stripe, tile_cols * 128),
            scratch(cls, stripe),
            scratch(2 * HALF, stripe),
            scratch(256, hid),
            scratch(8, 128, dtype=F32),
            scratch(128, 128, dtype=F32),
            scratch(ny, nx, 2, node_rows, f_in),
            scratch(ny, nx, 2, HALF, 128),
            scratch(tile_cols * 128, 256),
            scratch(nz, node_rows, f_in),
            scratch(nz, node_rows, f_in),
            scratch(2, node_rows, f_in),
            scratch(nz, HALF, 128),
            scratch(nz, HALF, 128),
            scratch(2, HALF, 128),
            scratch(ny, nx, 2, HALF, 128),
            scratch(ny, nx, HALF, 128),
            scratch(nx, ny, HALF, 128),
            scratch(nx, ny, HALF, 128),
            scratch(ny, HALF, 128),
            scratch(2, HALF, 128, dtype=F32),
            scratch(128, hid, dtype=F32),
            scratch(2, ny, nx * chunk, hid, dtype=F32),
            scratch(ny, nx * chunk, hid, dtype=F32),
            scratch(ny, nx * chunk, hid),
            scratch(ny, nx * chunk, hid),
            scratch(nx, chunk, hid, dtype=F32),
            scratch(nx, chunk, hid, dtype=F32),
            scratch(nz, 2 * chunk, hid // 2),
            scratch(2, ny, nx, chunk, hid, dtype=F32),
            sems(2),
            sems(19),
            sems(ny), sems(nx, ny // 2), sems(nx),
            sems(ny), sems(nx, ny // 2), sems(nx),
            sems(15),
        ],
        compiler_params=pltpu.CompilerParams(
            collective_id=0, has_side_effects=True, vmem_limit_bytes=48 * 1024 * 1024
        ),
    )(
        features, degrees.reshape(tile_rows, 128), tiles[0], table, w_first, w_second.T, cotangent.T
    )
    return logits, grad_first, grad_second.T


def solution(mesh):
    ny = 8 if mesh.shape["row"] == 64 else 2
    dims = (mesh.shape["row"] // (2 * ny), ny, mesh.shape["col"])
    placed = (
        P(("row", "col"), None),
        P("row"),
        P(("row", "col"), None, None, None),
        P(("row", "col"), None),
        P(("row", "col")),
        P(),
        P(),
        P("row", None),
    )
    return jax.shard_map(
        functools.partial(shards, dims),
        mesh=mesh,
        in_specs=placed,
        out_specs=(P(("row", "col"), None), P(), P()),
        check_vma=False,
    )
```

time: 124 us -> 98.6 us (0.80)
  Pallas kernels: 118 us -> 90.4 us
  local copies, waits for them, and re-layouts: 4.97 us -> 6.33 us
    pallas_call x1, Pallas kernels: 118 us -> 90.4 us  [shards(): pl.pallas_call(functools.partial(kernel, dims), out_shape=(jax.ShapeDtype...]
    unnamed x14 -> x17, local copies, waits for them, and re-layouts: 4.18 us -> 6.33 us
where the time goes in v2:
time: 98.6 us; the launch traced here: 98.2 us
  Pallas kernels  90.4 us (92%)
  local copies, waits for them, and re-layouts  6.33 us (6%)
  between operations  1.36 us (1%)
    pallas_call x1, Pallas kernels, shards(): pl.pallas_call(functools.partial(kernel, dims), out_shape=(jax.ShapeDtype...  90.4 us
    unnamed x17, local copies, waits for them, and re-layouts  6.33 us

profile of v2, /device:TPU:1, one launch (start us, length us, event | category | flops | bytes accessed | tf_op | source)
XLA Modules:
  0.0 98.2 jit_solution(7046819643477601028)
XLA Ops:
  0.6 0.0 copy-start.4
  1.3 0.0 copy-start.6
  1.3 0.0 copy-start.5
  1.3 0.6 copy-done.6
  2.0 0.1 select_reduce_fusion
  2.1 0.0 copy-done.4
  2.1 0.0 copy-done.5
  2.1 0.0 copy-start
  2.1 1.0 %copy-done = bf16[1,16,128,128]{3,2,1,0:T(8,128)(2,1)S(1)} copy-done((bf16[1,16,128,128]{3,2,1,0:T(8,128)(2,1)S(1)}, bf16[1,16,128,128]{3,2,1,0:T(8,128)(2,1)}, u32[]{:S(2)}) %copy-start) | copy-done | bytes 524312
  3.1 0.0 copy-start.1
  3.1 1.0 %copy-done.1 = bf16[1024,172]{0,1:T(8,128)(2,1)S(1)} copy-done((bf16[1024,172]{0,1:T(8,128)(2,1)S(1)}, bf16[1024,172]{0,1:T(8,128)(2,1)}, u32[]{:S(2)}) %copy-start.1) | copy-done | bytes 352280
  4.1 0.0 copy-start.2
  4.1 0.9 copy-done.2
  5.0 0.0 copy-start.3
  5.0 0.8 copy-done.3
  5.8 90.4 %shard_map.103 = (bf16[64,172]{1,0:T(8,128)(2,1)S(1)}, f32[128,256]{1,0:T(8,128)S(1)}, f32[172,256]{1,0:T(8,128)S(1)}) custom-call(bf16[64,128]{1,0:T(8,128)(2,1)S(1)} %copy-done.4, s32[8,128]{1,0:T(8,128)S(1)} %bitcast.12, bf16[16,128,128]{2,1,0:T(8,128)(2,1)S(1)} %bitcast.8, s32[256]{0:T(256)S(1)} %broadcast_add_fusion.table, ...), custom_call_target="tpu_custom_call" | custom-call | tf_op jit(solution)/shard_map/pallas_call | solution.py:411
  96.2 0.6 copy.15
  96.8 0.7 copy.16
  97.5 0.7 copy.17
  (3 shorter events, 0.0 us)
Async XLA Ops:
  0.6 1.4 %copy-start.4 = (bf16[64,128]{1,0:T(8,128)(2,1)S(1)}, bf16[64,128]{1,0:T(8,128)(2,1)}, u32[]{:S(2)}) copy-start(bf16[64,128]{1,0:T(8,128)(2,1)} %feat.1) | copy-start | bytes 49156
  1.3 0.7 copy-start.6
  1.3 0.8 copy-start.5
  2.1 1.0 %copy-start = (bf16[1,16,128,128]{3,2,1,0:T(8,128)(2,1)S(1)}, bf16[1,16,128,128]{3,2,1,0:T(8,128)(2,1)}, u32[]{:S(2)}) copy-start(bf16[1,16,128,128]{3,2,1,0:T(8,128)(2,1)} %param.10) | copy-start | bytes 1572868
  3.1 1.0 %copy-start.1 = (bf16[1024,172]{0,1:T(8,128)(2,1)S(1)}, bf16[1024,172]{0,1:T(8,128)(2,1)}, u32[]{:S(2)}) copy-start(bf16[1024,172]{0,1:T(8,128)(2,1)} %param.15) | copy-start | bytes 1056772
  4.1 0.9 copy-start.2
  5.0 0.8 copy-start.3

commit v3 on v2

--- a/solution.py
+++ b/solution.py
@@ -11,6 +11,7 @@
 F32, BF16 = jnp.float32, jnp.bfloat16
 CURVE = 0.7978845608028654
 CUBIC = 0.044715
+LIMIT = 63 * 1024 * 1024
 HALF = 96
 
 
@@ -31,10 +32,12 @@
 
 
 def kernel(
-    dims, feat, deg, tiles_hbm, table, w1, w2t, cot_hbm, logits, out_first, out_second,
-    tiles, adjacency, cot, scot, w2p, turned, own_scale,
+    dims, feat_hbm, deg_hbm, tiles_hbm, slots_hbm, counts_hbm, w1_hbm, w2t_hbm, cot_hbm,
+    logits, out_first, out_second,
+    feat, deg, tiles, slots_at, count_at, w1, w2t, cot, table_v, table,
+    adjacency, scot, w2p, own_scale,
     g1, g2, source, p1, r1, q1, p2, r2, q2, terms, sib, tsum, tx, ty, narrow_t, back_all,
-    grad, gsib, gys, gy, gxs, gx, gz, gfull,
+    grad, gsib, gys, gy, gxs, gx, gz, gw, gfull,
     local_sem, send_sem, g1y, g1x, g1s, g2y, g2x, g2s, one_sem,
 ):
     nx, ny, nz = dims
@@ -67,10 +70,13 @@
         if some:
             finish.append(lambda: await_bytes(ref, send_sem.at[send_id]))
 
-    tiles_copy = pltpu.make_async_copy(tiles_hbm, tiles.at[pl.ds(0, slots)], local_sem.at[0])
-    tiles_copy.start()
-    cot_copy = pltpu.make_async_copy(cot_hbm, cot, local_sem.at[1])
-    cot_copy.start()
+    def load(src, dst, i):
+        copy = pltpu.make_async_copy(src, dst, local_sem.at[i])
+        copy.start()
+        return copy
+
+    feat_copy, deg_copy = load(feat_hbm, feat, 0), load(deg_hbm, deg, 1)
+    slots_copy, count_copy = load(slots_hbm, slots_at, 2), load(counts_hbm, count_at, 3)
 
     barrier = pltpu.get_barrier_semaphore()
 
@@ -86,6 +92,11 @@
     @pl.loop(1, nz)
     def _(step):
         greet((row, lax.rem(z + step, nz)))
+
+    tiles_copy, cot_copy = load(tiles_hbm, tiles.at[pl.ds(0, slots)], 4), load(cot_hbm, cot, 5)
+    w1_copy, w2_copy = load(w1_hbm, w1, 6), load(w2t_hbm, w2t, 7)
+    feat_copy.wait()
+    deg_copy.wait()
 
     per_line = 128 // node_rows
     line = lax.rsqrt(deg[pl.ds(z // per_line, 1), :].astype(F32))
@@ -119,8 +130,9 @@
             for side in range(1, nx):
                 to = device(y, lax.rem(x + side, nx), core)
                 send(block, block, to, ids + 1, xsem.at[x, yy // 2])
-        column = g.at[:, x, core]
-        send(column, column, device(y, x, other), ids + 2, ssem.at[x])
+        for pair in range(pairs):
+            blocks = g.at[pl.ds(pair * 2, 2), x, core]
+            send(blocks, blocks, device(y, x, other), ids + 2, ssem.at[pair])
 
     def gather_columns(g, xsem, ssem, ids, steps):
         for step in steps:
@@ -129,23 +141,35 @@
                 xx = lax.rem(x + side, nx)
                 blocks = g.at[pl.ds(pair * 2, 2), xx, core]
                 await_bytes(blocks, xsem.at[xx, pair])
-                send(blocks, blocks, device(y, x, other), ids + 2, ssem.at[xx])
+                send(blocks, blocks, device(y, x, other), ids + 2, ssem.at[pair])
 
     pair_order = sorted(range(pairs), key=lambda step: min(step, pairs - step))
 
+    span = min(256, stripe)
+    peers, parts = span // node_rows, stripe // span
+
     def gather_finish(g, ssem):
-        for xx in range(nx):
-            await_bytes(g.at[:, xx, other], ssem.at[xx])
+        for pair in range(pairs):
+            await_bytes(g.at[pl.ds(pair * 2, 2), :, other], ssem.at[pair])
+
+    def unpack(first_line, lines, k):
+        @pl.loop(0, lines * nx)
+        def _(i):
+            line, xx = first_line + i // nx, lax.rem(i, nx)
+            block = g2[line, xx, k]
+            tail = block[node_rows:].astype(F32)
+            tail = jnp.concatenate([tail, pltpu.roll(tail, 64, 1)], axis=0).astype(BF16)
+            first = ((line * nx + xx) * 2 + k) * node_rows
+            rows = pl.ds(pl.multiple_of(first, node_rows), node_rows)
+            source[rows, :128] = block[:node_rows]
+            source[rows, 128:] = tail
 
     reach = nz // 4
 
-    def aggregate(source_of, pack, p, r, ids, sem, far_sem):
-        span = min(256, stripe)
-        peers, parts = span // node_rows, stripe // span
+    def aggregate(source_of, pack, p, r, ids, sem, far_sem, between=None):
         half = p.shape[1] // 2
 
-        @pl.loop(0, parts)
-        def _(i):
+        def one(i):
             part = i
             if parts == 4:
                 turn = (1 - i // 2) * (2 + i) + (i // 2) * (3 - i)
@@ -175,6 +199,11 @@
                         target = lax.rem(z + (2 * side - 1) * reach + nz, nz)
                         send(p.at[to, rows], r.at[4 * reach - 2, rows], (row, target), ids, one_sem.at[far_sem])
 
+        middle = parts // 2 if between else 0
+        if between:
+            pl.loop(0, middle)(one)
+            between()
+        pl.loop(middle, parts)(one)
         r[4 * reach - 1] = p[z]
         sent(r.at[pl.ds(0, nz - 1)], ids)
 
@@ -213,14 +242,24 @@
 
     gather_start(g1, g1y, g1x, 0)
 
+    slots_copy.wait()
+    count_copy.wait()
+    cells = lax.broadcasted_iota(jnp.int32, (8, 128), 0) * 128 + lax.broadcasted_iota(jnp.int32, (8, 128), 1)
+    count = count_at[0]
+    held = jnp.full((8, 128), slots, jnp.int32)
+    for t in range(slots):
+        held = jnp.where((cells == slots_at[0, t]) & (t < count), t, held)
+    table_v[...] = held
+    table_copy = load(table_v, table, 8)
     tiles_copy.wait()
     tiles[slots] = jnp.zeros((128, 128), BF16)
+    table_copy.wait()
 
     @pl.loop(0, tile_cols)
     def _(c):
         for r in range(tile_rows):
             adjacency[r * 128:(r + 1) * 128, pl.ds(pl.multiple_of(c * 128, 128), 128)] = tiles[
-                table[r * tile_cols + c]
+                table[r * tile_cols // 128, lax.rem(r * tile_cols, 128) + c]
             ]
 
     gather_rows(g1, g1y, g1x, g1s, 0)
@@ -232,6 +271,8 @@
         scot[:cls, r * 128:(r + 1) * 128] = (
             cot[:, r * 128:(r + 1) * 128].astype(F32) * by
         ).astype(BF16)
+    w1_copy.wait()
+    w2_copy.wait()
     w2p[cls // 16 * 16:, :] = jnp.zeros((w2p.shape[0] - cls // 16 * 16, w2p.shape[1]), BF16)
     w2p[:cls, :] = w2t[...]
 
@@ -296,9 +337,8 @@
     send(mine, mine, device(y, x, other), 18, one_sem.at[12])
     sent(mine, 18)
 
-    gather_rows(g2, g2y, g2x, g2s, 3)
-
     n_first, hid = out_first.shape
+    chunk = gz.shape[1]
     await_bytes(narrow_t.at[0], one_sem.at[12])
     lane_core = lax.broadcasted_iota(jnp.int32, (2 * HALF, 128), 1) // node_rows
     narrow = jnp.where(lane_core == core, narrow_t[...].reshape(2 * HALF, 128), 0.0)
@@ -310,7 +350,6 @@
     first_rows = dot(first_agg, grad_pre, ((0,), (0,)))
     hidden_twice = jnp.concatenate([hidden, hidden], axis=0)
     second_rows = dot(high, hidden_twice) + dot(low, hidden_twice)
-    chunk = gz.shape[1] // 2
     spare = 2 * nx * ny * chunk - n_first - 2 * HALF
     grad[...] = jnp.concatenate(
         [first_rows, second_rows, jnp.zeros((spare, hid), F32)], axis=0
@@ -318,7 +357,7 @@
     send(grad.at[other], gsib, device(y, x, other), 10, one_sem.at[4])
     sent(gsib, 10)
 
-    gather_columns(g2, g2x, g2s, 3, pair_order[:1])
+    gather_rows(g2, g2y, g2x, g2s, 3)
 
     await_bytes(gsib, one_sem.at[4])
     gys[...] = (gsib[...] + grad[core]).astype(BF16)
@@ -328,7 +367,12 @@
     sent(gy.at[pl.ds(0, ny - 1)], 11)
     gy[y] = gys[y]
 
-    gather_columns(g2, g2x, g2s, 3, pair_order[1:])
+    def second_columns(steps):
+        for step in steps:
+            gather_columns(g2, g2x, g2s, 3, [step])
+            unpack(lax.rem(y // 2 + step, pairs) * 2, 2, core)
+
+    second_columns(pair_order[:2])
 
     await_bytes(gy.at[pl.ds(0, ny - 1)], one_sem.at[5])
     gxs[...] = total(gy[i].astype(F32) for i in range(ny)).reshape(nx, chunk, hid)
@@ -338,38 +382,38 @@
     sent(gx.at[pl.ds(0, nx - 1)], 13, nx - 1)
     gx[x] = gxs[x]
 
+    second_columns(pair_order[2:])
+
+    await_bytes(gx.at[pl.ds(0, nx - 1)], one_sem.at[7])
+    group, member = z // 4, lax.rem(z, 4)
+    gz[member] = total(gx[i] for i in range(nx))
+    for step in range(1, 4):
+        to = group * 4 + lax.rem(member + step, 4)
+        send(gz.at[member], gz.at[member], (row, to), 14, one_sem.at[8])
+    sent(gz.at[pl.ds(0, 3)], 14)
+
     gather_finish(g2, g2s)
-
-    @pl.loop(0, tile_cols)
-    def _(i):
-        for k in range(2):
-            block = g2[i // nx, lax.rem(i, nx), k]
-            tail = block[node_rows:].astype(F32)
-            tail = jnp.concatenate([tail, pltpu.roll(tail, 64, 1)], axis=0).astype(BF16)
-            rows = pl.ds(pl.multiple_of(i * 128 + k * node_rows, node_rows), node_rows)
-            source[rows, :128] = block[:node_rows]
-            source[rows, 128:] = tail
-
-    await_bytes(gx.at[pl.ds(0, nx - 1)], one_sem.at[7])
-    summed = total(gx[i] for i in range(nx))
-    gz[z] = jnp.concatenate([summed[:, :128], summed[:, 128:]], axis=0).astype(BF16)
-
-    @pl.loop(1, nz)
-    def _(step):
-        send(gz.at[z], gz.at[z], (row, lax.rem(z + step, nz)), 14, one_sem.at[8])
-
-    sent(gz.at[pl.ds(0, nz - 1)], 14)
-
-    aggregate(lambda: source[...], pack_classes, p2, r2, 12, 6, 14)
+    unpack(0, ny, other)
+
+    groups = nz // 4
+    await_bytes(gz.at[pl.ds(0, 3)], one_sem.at[8])
+    gw[group] = total(gz[i] for i in range(4))
+    for step in range(1, groups):
+        to = lax.rem(group + step, groups) * 4 + member
+        send(gw.at[group], gw.at[group], (row, to), 19, one_sem.at[15])
+    sent(gw.at[pl.ds(0, groups - 1)], 19, groups - 1)
+
+    def spread_y():
+        await_bytes(gw.at[pl.ds(0, groups - 1)], one_sem.at[15])
+        gfull[core, y, x] = total(gw[i] for i in range(groups))
+        mine_y = gfull.at[core, y, x]
+        for step in y_order:
+            send(mine_y, mine_y, device(lax.rem(y + step, ny), x, core), 15, one_sem.at[9])
+        sent(gfull.at[0, pl.ds(0, ny - 1), 0], 15)
+
+    aggregate(lambda: source[...], pack_classes, p2, r2, 12, 6, 14, spread_y)
     relay(p2, r2, q2, 12, 6, 14)
 
-    await_bytes(gz.at[pl.ds(0, nz - 1)], one_sem.at[8])
-    summed = total(gz[i].astype(F32) for i in range(nz))
-    gfull[core, y, x] = jnp.concatenate([summed[:chunk], summed[chunk:]], axis=1)
-    mine_y = gfull.at[core, y, x]
-    for step in y_order:
-        send(mine_y, mine_y, device(lax.rem(y + step, ny), x, core), 15, one_sem.at[9])
-    sent(gfull.at[0, pl.ds(0, ny - 1), 0], 15)
     await_bytes(gfull.at[0, pl.ds(0, ny - 1), 0], one_sem.at[9])
     mine_x = gfull.at[core, :, x]
     for side in range(1, nx):
@@ -378,10 +422,6 @@
     await_bytes(gfull.at[0, :, pl.ds(0, nx - 1)], one_sem.at[10])
     send(gfull.at[core], gfull.at[core], device(y, x, other), 17, one_sem.at[11])
     sent(gfull.at[0], 17)
-    await_bytes(gfull.at[0], one_sem.at[11])
-    whole = gfull[...].reshape(2 * nx * ny * chunk, hid)
-    out_first[...] = whole[:n_first]
-    out_second[...] = whole[n_first:n_first + cls]
 
     packed = aggregate_sum(r2, 6)
     tail = packed[node_rows:]
@@ -389,7 +429,18 @@
     logits[:, :128] = (own * packed[:node_rows]).astype(BF16)
     logits[:, 128:] = (own * tail)[:, :cls - 128].astype(BF16)
 
+    await_bytes(gfull.at[0], one_sem.at[11])
+    whole = gfull[...].reshape(2 * nx * ny * chunk, hid)
+    out_first[...] = whole[:n_first]
+    out_second[...] = whole[n_first:n_first + cls]
+
     finish_all()
+
+
+def hand_out(a, b, c, a_out, b_out, c_out):
+    a_out[...] = a[...]
+    b_out[...] = b[...]
+    c_out[...] = c[...]
 
 
 def shards(dims, features, degrees, tiles, tile_slots, tile_counts, w_first, w_second, cotangent):
@@ -400,30 +451,33 @@
     stripe = nz * node_rows
     tile_rows, tile_cols = stripe // 128, ny * nx
     chunk = 512 // (2 * nx * ny)
-    cells = jnp.arange(tile_rows * tile_cols, dtype=jnp.int32)
-    order = jnp.arange(slots, dtype=jnp.int32)
-    hit = (tile_slots[0][None, :] == cells[:, None]) & (order < tile_counts[0])[None, :]
-    table = jnp.sum(jnp.where(hit, order - slots, 0), axis=1, dtype=jnp.int32) + slots
     vmem = pl.BlockSpec(memory_space=pltpu.VMEM)
-    far = pl.BlockSpec(memory_space=pl.ANY)
+    far = pl.BlockSpec(memory_space=pltpu.HBM)
     scratch = lambda *shape, dtype=BF16: pltpu.VMEM(shape, dtype)
     sems = lambda *shape: pltpu.SemaphoreType.DMA(shape)
-    logits, grad_first, grad_second = pl.pallas_call(
+    results = pl.pallas_call(
         functools.partial(kernel, dims),
         out_shape=(
             jax.ShapeDtypeStruct((node_rows, cls), BF16),
             jax.ShapeDtypeStruct((f_in, hid), F32),
             jax.ShapeDtypeStruct((cls, hid), F32),
         ),
-        in_specs=[vmem, vmem, far, pl.BlockSpec(memory_space=pltpu.SMEM), vmem, vmem, far],
+        in_specs=[far] * 8,
         out_specs=(vmem, vmem, vmem),
         scratch_shapes=[
+            scratch(node_rows, f_in),
+            scratch(tile_rows, 128, dtype=jnp.int32),
             scratch(slots + 1, 128, 128),
+            pltpu.SMEM((1, slots), jnp.int32),
+            pltpu.SMEM((1,), jnp.int32),
+            scratch(f_in, hid),
+            scratch(cls, hid),
+            scratch(cls, stripe),
+            scratch(8, 128, dtype=jnp.int32),
+            pltpu.SMEM((8, 128), jnp.int32),
             scratch(stripe, tile_cols * 128),
-            scratch(cls, stripe),
             scratch(2 * HALF, stripe),
             scratch(256, hid),
-            scratch(8, 128, dtype=F32),
             scratch(128, 128, dtype=F32),
             scratch(ny, nx, 2, node_rows, f_in),
             scratch(ny, nx, 2, HALF, 128),
@@ -447,20 +501,29 @@
             scratch(ny, nx * chunk, hid),
             scratch(nx, chunk, hid, dtype=F32),
             scratch(nx, chunk, hid, dtype=F32),
-            scratch(nz, 2 * chunk, hid // 2),
+            scratch(4, chunk, hid, dtype=F32),
+            scratch(nz // 4, chunk, hid, dtype=F32),
             scratch(2, ny, nx, chunk, hid, dtype=F32),
-            sems(2),
-            sems(19),
-            sems(ny), sems(nx, ny // 2), sems(nx),
-            sems(ny), sems(nx, ny // 2), sems(nx),
-            sems(15),
+            sems(9),
+            sems(20),
+            sems(ny), sems(nx, ny // 2), sems(ny // 2),
+            sems(ny), sems(nx, ny // 2), sems(ny // 2),
+            sems(16),
         ],
         compiler_params=pltpu.CompilerParams(
-            collective_id=0, has_side_effects=True, vmem_limit_bytes=48 * 1024 * 1024
+            collective_id=0, has_side_effects=True, vmem_limit_bytes=LIMIT
         ),
     )(
-        features, degrees.reshape(tile_rows, 128), tiles[0], table, w_first, w_second.T, cotangent.T
+        features, degrees.reshape(tile_rows, 128), tiles[0], tile_slots, tile_counts, w_first,
+        w_second.T, cotangent.T
     )
+    logits, grad_first, grad_second = pl.pallas_call(
+        hand_out,
+        out_shape=tuple(jax.ShapeDtypeStruct(a.shape, a.dtype) for a in results),
+        in_specs=[vmem] * 3,
+        out_specs=(vmem,) * 3,
+        compiler_params=pltpu.CompilerParams(vmem_limit_bytes=LIMIT),
+    )(*results)
     return logits, grad_first, grad_second.T
 
 

time: 98.6 us -> 94.3 us (0.956)
  local copies, waits for them, and re-layouts: 6.33 us -> 0 us
  Pallas kernels: 90.4 us -> 92.8 us
    unnamed x17 -> x0, local copies, waits for them, and re-layouts: 6.33 us -> none
    pallas_call x0 -> x1, Pallas kernels: none -> 1.74 us  [shards(): pl.pallas_call(hand_out, out_shape=tuple((jax.ShapeDtypeStruct(a.shape, a...]
where the time goes in v3:
time: 94.3 us; the launch traced here: 94.1 us
  Pallas kernels  92.8 us (98%)
  between operations  1.29 us (1%)
    pallas_call x1, Pallas kernels, shards(): pl.pallas_call(functools.partial(kernel, dims), out_shape=(jax.ShapeDtype...  91.1 us

profile of v3, /device:TPU:1, one launch (start us, length us, event | category | flops | bytes accessed | tf_op | source)
XLA Modules:
  0.0 94.1 jit_solution(738399272654904777)
XLA Ops:
  1.3 91.1 %shard_map.103 = (bf16[64,172]{1,0:T(8,128)(2,1)}, f32[128,256]{1,0:T(8,128)}, f32[172,256]{1,0:T(8,128)}) custom-call(bf16[64,128]{1,0:T(8,128)(2,1)} %feat_hbm.1, s32[8,128]{1,0:T(8,128)} %bitcast.8, bf16[16,128,128]{2,1,0:T(8,128)(2,1)} %bitcast.5, s32[1,16]{1,0:T(1,128)} %slots_hbm.1, s32[1]{0:T(128)S(6)} %copy.11.counts_hbm, bf16[128,256]{1,0:T(8,128)(2,1)} %w1_hbm.1, ...), custom_call_target="tpu_custom_call" | custom-call | tf_op jit(solution)/shard_map/pallas_call | solution.py:458
  92.4 1.7 %shard_map.104 = (bf16[64,172]{1,0:T(8,128)(2,1)}, f32[128,256]{1,0:T(8,128)}, f32[172,256]{1,0:T(8,128)}) custom-call(bf16[64,172]{1,0:T(8,128)(2,1)} %get-tuple-element.9.a, f32[128,256]{1,0:T(8,128)} %get-tuple-element.10.b, f32[172,256]{1,0:T(8,128)} %get-tuple-element.11.c), custom_call_target="tpu_custom_call" | custom-call | tf_op jit(solution)/shard_map/pallas_call | solution.py:520
